TPU v7x, 32 devices: a whole 2x2x4 slice. The times are simulated.
32 devices in a mesh: groups: 2 (over x), rows: 16 (over z, y, core).
Axes of the slice: x: 2, y: 2, z: 4, core: 2. Of those that a mesh axis runs over, the one named last changes fastest.
Arguments:
- tiles: bfloat16 [1024, 256, 256], P(('groups', 'rows')), parts along dimension 0, may hold values from -0.375 to 0.375
- tile_rows: int32 [1024], P(('groups', 'rows')), parts along dimension 0, may hold values from 0 to 3
- tile_cols: int32 [1024], P(('groups', 'rows')), parts along dimension 0, may hold values from 0 to 95, as said below
- tile_count: int32 [32], P(('groups', 'rows')), parts along dimension 0, may hold values from 16 to 32, as said below
- right_side: float32 [128, 256], P(('groups', 'rows')), parts along dimension 0, may hold values from -16 to 16
- row_kind: int32 [128, 256], P(('groups', 'rows')), parts along dimension 0, may hold values 0 or 1
- cost: float32 [192, 256], P(('groups', 'rows')), parts along dimension 0, may hold values from -16 to 16
- upper: float32 [192, 256], P(('groups', 'rows')), parts along dimension 0, may hold values from 0.05 to 2
- primal_init: float32 [192, 256], P(('groups', 'rows')), parts along dimension 0, may hold values from 0 to 1
- dual_init: float32 [128, 256], P(('groups', 'rows')), parts along dimension 0, may hold values from -3 to 3
Outputs:
- primal: float32 [192, 256], P(('groups', 'rows')), parts along dimension 0
- dual: float32 [128, 256], P(('groups', 'rows')), parts along dimension 0
- norms: float32 [4, 2], P('groups'), parts along dimension 0
There are 2 independent parts, one for each index of `groups`. A program takes and returns all parts, laid end to end along the dimension named above; each array names one. Nothing has to cross between parts.
Inputs may be any that keep to these rules, and one draw needn't show every extreme that they name: `tile_count`: some device-block has all 32 tiles live. `tile_cols`: of the tiles of one device-block, at most 2 have column blocks among one device-block's 6 columns (c // 6 equal); every device-block reaches 2 for some such column device-block, and every column device-block receives 2 from some device-block.
All inputs are finite; a program needn't handle non-finite values. No bound on the sum of `row_kind` on one device may be relied on, other than what follows from the above.
Results may differ from a plain program's by a relative error of at most 0.00073.
Values may be sent and summed in bfloat16 or wider, within the bound.
A program may use at most 64 MiB of HBM per device.

v0:
```python
import jax
import jax.numpy as jnp
from jax import lax
from jax.sharding import PartitionSpec as P

ITERS = 2


primal_step = 0.1
dual_step = 0.1


def per_device(
    tiles,
    tile_rows,
    tile_cols,
    tile_count,
    right_side,
    row_kind,
    cost,
    upper,
    primal_init,
    dual_init,
):
    slots = tiles.shape[0]
    row_count = right_side.shape[0]
    col_count = cost.shape[0]
    devices = lax.axis_size("rows")
    col_total = col_count * devices
    live = (jnp.arange(slots, dtype=jnp.int32) < tile_count[0]).astype(jnp.float32)
    row_select = tile_rows[:, None] == jnp.arange(row_count, dtype=jnp.int32)[None, :]
    row_select_f = row_select.astype(jnp.float32)
    row_select_b = row_select.astype(jnp.bfloat16)
    bounded = row_kind == 1

    def forward(picked):
        parts = (
            jnp.einsum("tij,tj->ti", tiles, picked, preferred_element_type=jnp.float32)
            * live[:, None]
        )
        return jnp.dot(row_select_f.T, parts, precision=lax.Precision.HIGHEST)

    def adjoint_parts(dual_b):
        picked = jnp.dot(row_select_b, dual_b, preferred_element_type=jnp.float32).astype(
            jnp.bfloat16
        )
        return (
            jnp.einsum("tij,ti->tj", tiles, picked, preferred_element_type=jnp.float32)
            * live[:, None]
        )

    capacity = -(-slots // devices)
    owner_dev = tile_cols // col_count
    local_col = tile_cols % col_count
    order = jnp.arange(slots, dtype=jnp.int32)
    earlier = (owner_dev[:, None] == owner_dev[None, :]) & (order[None, :] < order[:, None])
    rank = jnp.sum(earlier.astype(jnp.int32), axis=1)
    target = owner_dev * capacity + rank
    send_select = target[None, :] == jnp.arange(devices * capacity, dtype=jnp.int32)[:, None]
    send_f = send_select.astype(jnp.float32)
    pick_b = send_select.T.astype(jnp.bfloat16)
    send_cols = jnp.max(jnp.where(send_select, local_col[None, :], -1), axis=1).astype(jnp.float32)
    requests = lax.all_to_all(send_cols, "rows", split_axis=0, concat_axis=0, tiled=True)
    col_range = jnp.arange(col_count, dtype=jnp.float32)
    reply_select = (requests[:, None] == col_range[None, :]).astype(jnp.bfloat16)

    def spread_primal(vector_b):
        reply = jnp.dot(reply_select, vector_b, preferred_element_type=jnp.float32).astype(
            jnp.bfloat16
        )
        back = lax.all_to_all(reply, "rows", split_axis=0, concat_axis=0, tiled=True)
        return jnp.dot(pick_b, back, preferred_element_type=jnp.float32).astype(jnp.bfloat16)

    def column_image(dual_b):
        parts = adjoint_parts(dual_b)
        outgoing = jnp.dot(send_f, parts, precision=lax.Precision.HIGHEST)
        arrived, arrived_cols = (
            lax.all_to_all(outgoing, "rows", split_axis=0, concat_axis=0, tiled=True),
            lax.all_to_all(send_cols, "rows", split_axis=0, concat_axis=0, tiled=True),
        )
        place = (arrived_cols[None, :] == col_range[:, None]).astype(jnp.float32)
        return jnp.dot(place, arrived, precision=lax.Precision.HIGHEST)

    primal_x, cost_here, upper_here = (primal_init, cost, upper)
    dual_y = dual_init
    row_image = forward(spread_primal(primal_x.astype(jnp.bfloat16)))
    col_image = column_image(dual_y.astype(jnp.bfloat16))
    row_scale = 1.0 / (row_count * devices * right_side.shape[1])
    col_scale = 1.0 / (col_total * cost.shape[1])
    results = []
    for step in range(ITERS):
        x_new = jnp.clip(primal_x - primal_step * (cost_here - col_image), 0.0, upper_here)
        x_bar = (2.0 * x_new - primal_x).astype(jnp.bfloat16)
        bar_image = forward(spread_primal(x_bar))
        row_image = (bar_image + row_image) / 2.0
        y_new = dual_y + dual_step * (right_side - bar_image)
        y_new = jnp.where(bounded, jnp.maximum(y_new, 0.0), y_new)
        violation = right_side - row_image
        violation = jnp.where(bounded, jnp.maximum(violation, 0.0), violation)
        primal_term = jnp.sum(violation * violation)
        primal_sum = lax.psum(primal_term, "rows")
        col_image = column_image(y_new.astype(jnp.bfloat16))
        gap = x_new - jnp.clip(x_new - (cost_here - col_image), 0.0, upper_here)
        dual_term = jnp.sum(gap * gap)
        dual_sum = lax.psum(dual_term, "rows")
        results.append(
            jnp.stack([jnp.sqrt(primal_sum * row_scale), jnp.sqrt(dual_sum * col_scale)])
        )
        primal_x = x_new
        dual_y = y_new
    norms = jnp.stack(results)
    return (primal_x, dual_y, norms)


def solution(mesh):
    return jax.shard_map(
        per_device,
        mesh=mesh,
        in_specs=(
            P(("groups", "rows"), None, None),
            P(("groups", "rows")),
            P(("groups", "rows")),
            P(("groups", "rows")),
            P(("groups", "rows"), None),
            P(("groups", "rows"), None),
            P(("groups", "rows"), None),
            P(("groups", "rows"), None),
            P(("groups", "rows"), None),
            P(("groups", "rows"), None),
        ),
        out_specs=(P(("groups", "rows"), None), P(("groups", "rows"), None), P("groups", None)),
        check_vma=False,
    )
```

profile of v0, /device:TPU:0, one launch (start us, length us, event | category | flops | bytes accessed | tf_op | source)
XLA Modules:
  0.0 124.8 jit_solution(7256608120139581940)
XLA Ops:
  0.7 0.7 and_select_fusion
  1.7 0.7 convert_element_type.78
  2.4 7.4 %all-to-all-start = ((f32[16,2,1]{1,2,0:T(1,128)}), f32[16,2,1]{1,2,0:T(1,128)S(1)}, u32[]{:S(2)}, u32[]{:S(2)}) async-start(f32[16,2,1]{1,2,0:T(1,128)} %bitcast), calls=%async_computation | async-start | bytes 16384 | tf_op jit(solution)/shard_map/all_to_all | solution.py:79
  10.4 0.9 fusion
  11.3 2.9 %fusion.38 = f32[32,1,256]{2,1,0:T(1,128)S(1)} fusion(bf16[32,256,256]{2,1,0:T(8,128)(2,1)} %param.10, bf16[32,256,1]{1,0,2:T(8,128)(2,1)S(1)} %fusion), kind=kOutput, calls=%fused_computation.57 | convolution fusion | flops 4194304 | bytes 4243456 | tf_op jit(solution)/shard_map/tij,ti->tj/dot_general | solution.py:48
  14.4 0.6 all_to_all.56
  15.1 1.0 all-to-all-done
  16.1 5.0 %all-to-all-start.1 = ((f32[16,2,256]{2,1,0:T(2,128)}), f32[16,2,256]{2,1,0:T(2,128)S(1)}, u32[]{:S(2)}, u32[]{:S(2)}) async-start(f32[16,2,256]{2,1,0:T(2,128)} %all_to_all.56), calls=%async_computation.1 | async-start | bytes 65536 | tf_op jit(solution)/shard_map/all_to_all | solution.py:78
  21.6 0.7 reduce.3
  22.6 0.6 all_to_all.68
  23.2 4.5 %all-to-all-done.1 = f32[16,2,256]{2,1,0:T(2,128)S(1)} async-done(((f32[16,2,256]{2,1,0:T(2,128)}), f32[16,2,256]{2,1,0:T(2,128)S(1)}, u32[]{:S(2)}, u32[]{:S(2)}) %all-to-all-start.1) | async-done | bytes 32800 | tf_op jit(solution)/shard_map/all_to_all | solution.py:78
  27.7 3.5 %all-to-all-start.5 = ((bf16[16,2,256]{2,1,0:T(2,128)(2,1)}), bf16[16,2,256]{2,1,0:T(2,128)(2,1)S(1)}, u32[]{:S(2)}, u32[]{:S(2)}) async-start(bf16[16,2,256]{2,1,0:T(2,128)(2,1)} %all_to_all.68), calls=%async_computation.5 | async-start | bytes 32768 | tf_op jit(solution)/shard_map/all_to_all | solution.py:71
  31.6 0.6 all_to_all.59
  32.2 5.5 %all-to-all-done.5 = bf16[16,2,256]{2,1,0:T(2,128)(2,1)S(1)} async-done(((bf16[16,2,256]{2,1,0:T(2,128)(2,1)}), bf16[16,2,256]{2,1,0:T(2,128)(2,1)S(1)}, u32[]{:S(2)}, u32[]{:S(2)}) %all-to-all-start.5) | async-done | bytes 16416 | tf_op jit(solution)/shard_map/all_to_all | solution.py:71
  37.7 3.5 %all-to-all-start.2 = ((bf16[16,2,256]{2,1,0:T(2,128)(2,1)}), bf16[16,2,256]{2,1,0:T(2,128)(2,1)S(1)}, u32[]{:S(2)}, u32[]{:S(2)}) async-start(bf16[16,2,256]{2,1,0:T(2,128)(2,1)} %all_to_all.59), calls=%async_computation.2 | async-start | bytes 32768 | tf_op jit(solution)/shard_map/all_to_all | solution.py:71
  41.2 6.4 %all-to-all-done.2 = bf16[16,2,256]{2,1,0:T(2,128)(2,1)S(1)} async-done(((bf16[16,2,256]{2,1,0:T(2,128)(2,1)}), bf16[16,2,256]{2,1,0:T(2,128)(2,1)S(1)}, u32[]{:S(2)}, u32[]{:S(2)}) %all-to-all-start.2) | async-done | bytes 16416 | tf_op jit(solution)/shard_map/all_to_all | solution.py:71
  47.8 3.5 %fusion.35 = f32[32,1,256]{2,1,0:T(1,128)S(1)} fusion(bf16[32,256,256]{2,1,0:T(8,128)(2,1)} %param.10, bf16[32,256,1]{1,0,2:T(8,128)(2,1)S(1)} %fusion.1), kind=kOutput, calls=%fused_computation.54 | convolution fusion | flops 4194304 | bytes 4243456 | tf_op jit(solution)/shard_map/tij,tj->ti/dot_general | solution.py:38
  51.8 0.7 fusion.32
  52.7 0.6 all_to_all.62
  53.3 3.5 %all-to-all-start.3 = ((f32[16,2,256]{2,1,0:T(2,128)}), f32[16,2,256]{2,1,0:T(2,128)S(1)}, u32[]{:S(2)}, u32[]{:S(2)}) async-start(f32[16,2,256]{2,1,0:T(2,128)} %all_to_all.62), calls=%async_computation.3 | async-start | bytes 65536 | tf_op jit(solution)/shard_map/all_to_all | solution.py:78
  57.0 6.4 %all-to-all-done.3 = f32[16,2,256]{2,1,0:T(2,128)S(1)} async-done(((f32[16,2,256]{2,1,0:T(2,128)}), f32[16,2,256]{2,1,0:T(2,128)S(1)}, u32[]{:S(2)}, u32[]{:S(2)}) %all-to-all-start.3) | async-done | bytes 32800 | tf_op jit(solution)/shard_map/all_to_all | solution.py:78
  63.4 0.7 multiply_reduce_fusion
  64.4 0.6 all_to_all.65
  65.0 3.4 %all-to-all-start.4 = ((bf16[16,2,256]{2,1,0:T(2,128)(2,1)}), bf16[16,2,256]{2,1,0:T(2,128)(2,1)S(1)}, u32[]{:S(2)}, u32[]{:S(2)}) async-start(bf16[16,2,256]{2,1,0:T(2,128)(2,1)} %all_to_all.65), calls=%async_computation.4 | async-start | bytes 32768 | tf_op jit(solution)/shard_map/all_to_all | solution.py:71
  68.4 3.4 %fusion.26 = f32[32,1,256]{2,1,0:T(1,128)S(1)} fusion(bf16[32,256,256]{2,1,0:T(8,128)(2,1)} %param.10, bf16[32,256,1]{1,0,2:T(8,128)(2,1)S(1)} %fusion.4), kind=kOutput, calls=%fused_computation.45 | convolution fusion | flops 4194304 | bytes 4243456 | tf_op jit(solution)/shard_map/tij,tj->ti/dot_general | solution.py:38
  71.8 3.1 %all-to-all-done.4 = bf16[16,2,256]{2,1,0:T(2,128)(2,1)S(1)} async-done(((bf16[16,2,256]{2,1,0:T(2,128)(2,1)}), bf16[16,2,256]{2,1,0:T(2,128)(2,1)S(1)}, u32[]{:S(2)}, u32[]{:S(2)}) %all-to-all-start.4) | async-done | bytes 16416 | tf_op jit(solution)/shard_map/all_to_all | solution.py:71
  75.1 3.5 %fusion.29 = f32[32,1,256]{2,1,0:T(1,128)S(1)} fusion(bf16[32,256,256]{2,1,0:T(8,128)(2,1)} %param.10, bf16[32,256,1]{1,0,2:T(8,128)(2,1)S(1)} %fusion.3), kind=kOutput, calls=%fused_computation.48 | convolution fusion | flops 4194304 | bytes 4243456 | tf_op jit(solution)/shard_map/tij,tj->ti/dot_general | solution.py:38
  78.9 0.9 fusion.63
  80.0 0.7 fusion.23
  80.9 9.3 %all_to_all.81 = f32[16,2,256]{2,1,0:T(2,128)S(1)} all-to-all(f32[16,2,256]{2,1,0:T(2,128)S(1)} %all_to_all.71), channel_id=1, replica_groups=mesh['groups'=2,'rows'=16] {'rows'}, dimensions={0} | all-to-all | bytes 65536 | tf_op jit(solution)/shard_map/all_to_all | solution.py:78
  90.3 0.8 fusion.16
  91.1 30.3 %all-reduce = (f32[]{:T(128)}, f32[]{:T(128)}, f32[]{:T(128)}, f32[]{:T(128)}) all-reduce(f32[]{:T(128)} %fusion.16, f32[]{:T(128)} %get-tuple-element.4, f32[]{:T(128)} %get-tuple-element.9, f32[]{:T(128)} %get-tuple-element.3), channel_id=1, replica_groups=mesh['groups'=2,'rows'=16] {'rows'}, use_global_device_ids=true, to_apply=%region_9.10 | all-reduce | flops 4 | bytes 32 | tf_op jit(solution)/shard_map/psum | solution.py:105
  (53 shorter events, 4.6 us)
Async XLA Ops:
  0.6 21.7 %copy-start.5 = (f32[6,256]{1,0:T(8,128)S(1)}, f32[6,256]{1,0:T(8,128)}, u32[]{:S(2)}) copy-start(f32[6,256]{1,0:T(8,128)} %param.18) | copy-start | bytes 18436
  0.6 30.6 %copy-start.3 = (f32[6,256]{1,0:T(8,128)S(1)}, f32[6,256]{1,0:T(8,128)}, u32[]{:S(2)}) copy-start(f32[6,256]{1,0:T(8,128)} %param.16) | copy-start | bytes 18436
  0.7 30.6 %copy-start.2 = (f32[6,256]{1,0:T(8,128)S(1)}, f32[6,256]{1,0:T(8,128)}, u32[]{:S(2)}) copy-start(f32[6,256]{1,0:T(8,128)} %param.17) | copy-start | bytes 18436
  0.7 40.5 %copy-start.6 = (s32[4,256]{1,0:T(4,128)S(1)}, s32[4,256]{1,0:T(4,128)}, u32[]{:S(2)}) copy-start(s32[4,256]{1,0:T(4,128)} %param.15) | copy-start | bytes 12292
  2.4 13.7 %all-to-all-start = ((f32[16,2,1]{1,2,0:T(1,128)}), f32[16,2,1]{1,2,0:T(1,128)S(1)}, u32[]{:S(2)}, u32[]{:S(2)}) async-start(f32[16,2,1]{1,2,0:T(1,128)} %bitcast), calls=%async_computation | async-start | bytes 16384 | tf_op jit(solution)/shard_map/all_to_all | solution.py:79
  11.3 40.0 %copy-start.9 = (s32[32]{0:T(128)S(1)}, s32[32]{0:T(128)}, u32[]{:S(2)}) copy-start(s32[32]{0:T(128)} %param.11) | copy-start | bytes 388
  11.3 40.3 %copy-start.7 = (f32[4,256]{1,0:T(4,128)S(1)}, f32[4,256]{1,0:T(4,128)}, u32[]{:S(2)}) copy-start(f32[4,256]{1,0:T(4,128)} %param.19) | copy-start | bytes 12292
  11.3 40.3 %copy-start.8 = (f32[4,256]{1,0:T(4,128)S(1)}, f32[4,256]{1,0:T(4,128)}, u32[]{:S(2)}) copy-start(f32[4,256]{1,0:T(4,128)} %param.14) | copy-start | bytes 12292
  16.1 11.6 %all-to-all-start.1 = ((f32[16,2,256]{2,1,0:T(2,128)}), f32[16,2,256]{2,1,0:T(2,128)S(1)}, u32[]{:S(2)}, u32[]{:S(2)}) async-start(f32[16,2,256]{2,1,0:T(2,128)} %all_to_all.56), calls=%async_computation.1 | async-start | bytes 65536 | tf_op jit(solution)/shard_map/all_to_all | solution.py:78
  27.7 10.0 %all-to-all-start.5 = ((bf16[16,2,256]{2,1,0:T(2,128)(2,1)}), bf16[16,2,256]{2,1,0:T(2,128)(2,1)S(1)}, u32[]{:S(2)}, u32[]{:S(2)}) async-start(bf16[16,2,256]{2,1,0:T(2,128)(2,1)} %all_to_all.68), calls=%async_computation.5 | async-start | bytes 32768 | tf_op jit(solution)/shard_map/all_to_all | solution.py:71
  37.7 9.9 %all-to-all-start.2 = ((bf16[16,2,256]{2,1,0:T(2,128)(2,1)}), bf16[16,2,256]{2,1,0:T(2,128)(2,1)S(1)}, u32[]{:S(2)}, u32[]{:S(2)}) async-start(bf16[16,2,256]{2,1,0:T(2,128)(2,1)} %all_to_all.59), calls=%async_computation.2 | async-start | bytes 32768 | tf_op jit(solution)/shard_map/all_to_all | solution.py:71
  47.6 4.2 %copy-start = (bf16[32,256,256]{2,1,0:T(8,128)(2,1)S(1)}, bf16[32,256,256]{2,1,0:T(8,128)(2,1)}, u32[]{:S(2)}) copy-start(bf16[32,256,256]{2,1,0:T(8,128)(2,1)} %param.10) | copy-start | bytes 12582916
  53.3 10.1 %all-to-all-start.3 = ((f32[16,2,256]{2,1,0:T(2,128)}), f32[16,2,256]{2,1,0:T(2,128)S(1)}, u32[]{:S(2)}, u32[]{:S(2)}) async-start(f32[16,2,256]{2,1,0:T(2,128)} %all_to_all.62), calls=%async_computation.3 | async-start | bytes 65536 | tf_op jit(solution)/shard_map/all_to_all | solution.py:78
  64.2 26.1 %copy-start.4 = (f32[6,256]{1,0:T(8,128)}, f32[6,256]{1,0:T(8,128)S(1)}, u32[]{:S(2)}) copy-start(f32[6,256]{1,0:T(8,128)S(1)} %get-tuple-element.10) | copy-start | bytes 18436
  65.0 9.9 %all-to-all-start.4 = ((bf16[16,2,256]{2,1,0:T(2,128)(2,1)}), bf16[16,2,256]{2,1,0:T(2,128)(2,1)S(1)}, u32[]{:S(2)}, u32[]{:S(2)}) async-start(bf16[16,2,256]{2,1,0:T(2,128)(2,1)} %all_to_all.65), calls=%async_computation.4 | async-start | bytes 32768 | tf_op jit(solution)/shard_map/all_to_all | solution.py:71
  74.9 5.1 %copy-start.1 = (bf16[32,256,256]{2,1,0:T(8,128)(2,1)S(1)}, bf16[32,256,256]{2,1,0:T(8,128)(2,1)}, u32[]{:S(2)}) copy-start(bf16[32,256,256]{2,1,0:T(8,128)(2,1)} %param.10) | copy-start | bytes 12582916
  79.8 45.0 %copy-start.10 = (f32[4,256]{1,0:T(4,128)}, f32[4,256]{1,0:T(4,128)S(1)}, u32[]{:S(2)}) copy-start(f32[4,256]{1,0:T(4,128)S(1)} %get-tuple-element.11) | copy-start | bytes 12292
where the time goes:
time: 126 us; the launch traced here: 125 us
  blocking collectives  39.7 us (32%)
  waiting for transfers between devices  26.9 us (21%)
  starting transfers between devices  26.2 us (21%)
  matrix products  20.7 us (16%)
  local copies, waits for them, and re-layouts  4.58 us (4%)
  between operations  4.3 us (3%)
  other arithmetic  2.33 us (2%)
    psum x1, blocking collectives, per_device(): dual_sum = lax.psum(dual_term, 'rows')  30.3 us
    all_to_all x3, waiting for transfers between devices, spread_primal(): lax.all_to_all(reply, 'rows', split_axis=0, concat_axis=0, tiled=True)  15 us
    all_to_all x2, waiting for transfers between devices, column_image(): lax.all_to_all(outgoing, 'rows', split_axis=0, concat_axis=0, tiled=True)  10.9 us
    dot_general x3, matrix products, forward(): jnp.einsum('tij,tj->ti', tiles, picked, preferred_element_type=jnp.float32)  10.4 us
    all_to_all x3, starting transfers between devices, spread_primal(): lax.all_to_all(reply, 'rows', split_axis=0, concat_axis=0, tiled=True)  10.4 us
    all_to_all x1, blocking collectives, column_image(): lax.all_to_all(outgoing, 'rows', split_axis=0, concat_axis=0, tiled=True)  9.33 us
    all_to_all x2, starting transfers between devices, column_image(): lax.all_to_all(outgoing, 'rows', split_axis=0, concat_axis=0, tiled=True)  8.46 us
    all_to_all x1, starting transfers between devices, column_image(): lax.all_to_all(send_cols, 'rows', split_axis=0, concat_axis=0, tiled=True)  7.39 us
  transfers between devices with their start and end apart: 6, of which 6 were waited for; matrix products, arithmetic and copies ran while one was open for 7% of the time, Pallas kernels for 0%

commit v1 on v0

v1 whole, which is shorter than its diff:
```python
import functools

import jax
import jax.numpy as jnp
from jax import lax
from jax.experimental import pallas as pl
from jax.experimental.pallas import tpu as pltpu
from jax.sharding import PartitionSpec as P

ITERS = 2
PRIMAL_STEP = 0.1
DUAL_STEP = 0.1
LANES = 128
MSG = 8
CHUNKS = 4
MESH = pl.DeviceIdType.MESH


def kernel(
    devices,
    rows_s,
    cols_s,
    count_s,
    tiles_h,
    right_h,
    kind_h,
    cost_h,
    upper_h,
    x_h,
    y_h,
    x_out,
    y_out,
    norm_out,
    tiles_v,
    right_v,
    kind_v,
    cost_v,
    upper_v,
    x_v,
    y_v,
    yb_v,
    peer_v,
    base_v,
    target_v,
    pick_v,
    send,
    recv,
    small_sem,
    tile_sem,
    send_sem,
    recv_sem,
):
    slots, block = tiles_v.shape[0], tiles_v.shape[1]
    row_count, col_count = right_v.shape[0], cost_v.shape[0]
    halves = block // LANES
    capacity = -(-slots // devices)
    per_vector = halves * capacity
    places = devices * capacity
    span = MSG * devices
    per_chunk = slots // CHUNKS
    me = lax.axis_index("rows")

    def peer_of(step):
        return lax.rem(me + step, devices)

    def each_peer(do):
        if devices <= 16:
            for step in range(1, devices):
                do(step)
        else:
            pl.loop(1, devices)(do)

    chunk_copies = []
    for c in range(CHUNKS):
        part = pl.ds(c * per_chunk, per_chunk)
        chunk_copies.append(
            pltpu.make_async_copy(tiles_h.at[part], tiles_v.at[part], tile_sem.at[c])
        )
    small_copies = []
    pairs = (
        (y_h, y_v),
        (cost_h, cost_v),
        (upper_h, upper_v),
        (x_h, x_v),
        (right_h, right_v),
        (kind_h, kind_v),
    )
    for n, (src, dst) in enumerate(pairs):
        small_copies.append(pltpu.make_async_copy(src, dst, small_sem.at[n]))
    small_copies[0].start()
    for copy in chunk_copies:
        copy.start()
    for copy in small_copies[1:]:
        copy.start()

    barrier = pltpu.get_barrier_semaphore()

    def greet(step):
        pl.semaphore_signal(
            barrier, inc=1, device_id={"rows": peer_of(step)}, device_id_type=MESH
        )

    each_peer(greet)

    lane = lax.broadcasted_iota(jnp.int32, (slots, LANES), 1)
    sub = lax.broadcasted_iota(jnp.int32, (slots, LANES), 0)
    lane1 = lax.broadcasted_iota(jnp.int32, (1, LANES), 1)
    peer_l = jnp.full((1, LANES), -1, jnp.int32)
    local_l = jnp.zeros((1, LANES), jnp.int32)
    for t in range(slots):
        col = cols_s[t]
        owner = col // col_count
        local = col - owner * col_count
        step = owner - me
        step = jnp.where(step < 0, step + devices, step)
        step = jnp.where(t < count_s[0], step, 16 * devices + t)
        peer_v[t : t + 1, :] = jnp.full((1, LANES), step, jnp.int32)
        peer_l = jnp.where(lane1 == t, step, peer_l)
        local_l = jnp.where(lane1 == t, local, local_l)
    peer_s = peer_v[...]
    same = peer_s == peer_l
    rank_s = jnp.sum(jnp.where(same & (lane < sub), 1.0, 0.0), axis=1, keepdims=True)
    rank_l = jnp.sum(jnp.where(same & (sub < lane), 1.0, 0.0), axis=0, keepdims=True)
    rank_s = rank_s.astype(jnp.int32)
    base_v[...] = peer_s * MSG + rank_s
    target_v[...] = peer_s + rank_s * devices
    target_l = peer_l + rank_l.astype(jnp.int32) * devices

    place = lax.broadcasted_iota(jnp.int32, (places, LANES), 0)
    found = (target_l == place) & (
        lax.broadcasted_iota(jnp.int32, (places, LANES), 1) < slots
    )
    col_of = jnp.sum(
        jnp.where(found, (local_l + 1).astype(jnp.float32), 0.0), axis=1, keepdims=True
    )
    col_of = jnp.broadcast_to(col_of - 1.0, (places, LANES))
    send[...] = jnp.zeros_like(send)
    for s in range(capacity):
        send[0, pl.ds(per_vector + s, devices, stride=MSG), :] = col_of[
            s * devices : (s + 1) * devices
        ]

    wide_lane = lax.broadcasted_iota(jnp.int32, (16, span), 1)
    wide_sub = lax.broadcasted_iota(jnp.int32, (16, span), 0)
    vector_of = wide_sub // row_count
    row_of = jnp.where(vector_of < 2, wide_sub - vector_of * row_count, -1)
    wanted = wide_lane - vector_of * per_vector
    for t in range(slots):
        base = base_v[t : t + 1, :]
        if span > LANES:
            base = jnp.concatenate([base] * (span // LANES), axis=1)
        hit_row = row_of == rows_s[t]
        for h in range(halves):
            hit = hit_row & (wanted == base + h * capacity)
            pick_v[h, t * 16 : (t + 1) * 16, :] = jnp.where(hit, 1.0, 0.0).astype(
                jnp.bfloat16
            )

    place_wide = lax.broadcasted_iota(jnp.int32, (places, block), 0)

    def adjoint(first):
        total = jnp.zeros((places, block), jnp.float32)
        for c in range(CHUNKS):
            if first:
                chunk_copies[c].wait()
            parts = []
            for t in range(c * per_chunk, (c + 1) * per_chunk):
                row = yb_v[pl.ds(rows_s[t], 1), :]
                target = target_v[t : t + 1, :]
                target = jnp.concatenate([target] * halves, axis=1)
                parts.append(
                    jnp.where(target == place_wide, row, 0.0).astype(jnp.bfloat16)
                )
            left = jnp.concatenate(parts, axis=1)
            right = tiles_v[c * per_chunk : (c + 1) * per_chunk].reshape(
                per_chunk * block, block
            )
            total += jnp.dot(left, right, preferred_element_type=jnp.float32)
        return total

    def forward(e):
        arrived = recv[e].astype(jnp.bfloat16)
        picked = [
            jnp.dot(pick_v[h], arrived, preferred_element_type=jnp.float32).astype(
                jnp.bfloat16
            )
            for h in range(halves)
        ]
        total = jnp.zeros((16, block), jnp.float32)
        for t in range(slots):
            left = jnp.concatenate([p[t * 16 : (t + 1) * 16] for p in picked], axis=1)
            total += lax.dot_general(
                left, tiles_v[t], (((1,), (1,)), ((), ())), preferred_element_type=jnp.float32
            )
        return total

    def exchange(e):
        recv[e, 0:MSG, :] = send[e, 0:MSG, :]

        def go(step):
            pltpu.make_async_remote_copy(
                src_ref=send.at[e, pl.ds(pl.multiple_of(MSG * step, MSG), MSG)],
                dst_ref=recv.at[e, pl.ds(pl.multiple_of(MSG * (devices - step), MSG), MSG)],
                send_sem=send_sem.at[e],
                recv_sem=recv_sem.at[e],
                device_id={"rows": peer_of(step)},
                device_id_type=MESH,
            ).start()

        each_peer(go)

    def settle(buffer, sems, e):
        rest = buffer.at[e, pl.ds(MSG, span - MSG)]
        pltpu.make_async_copy(rest, rest, sems.at[e]).wait()

    def send_terms(e, terms):
        for s in range(capacity):
            for h in range(halves):
                send[e, pl.ds(h * capacity + s, devices, stride=MSG), :] = terms[
                    s * devices : (s + 1) * devices, h * LANES : (h + 1) * LANES
                ]
        exchange(e)

    sub8 = lax.broadcasted_iota(jnp.int32, (MSG, LANES), 0).astype(jnp.float32)

    def column_image(e):
        sums = [[jnp.zeros((MSG, LANES), jnp.float32) for _ in range(2)] for _ in range(halves)]
        count = 0
        for k in range(devices):
            for s in range(capacity):
                at = k * MSG + per_vector + s
                hit = recv[0, at : at + 1, :] == sub8
                for h in range(halves):
                    at = k * MSG + h * capacity + s
                    term = jnp.where(hit, recv[e, at : at + 1, :], 0.0)
                    sums[h][count % 2] += term
                count += 1
        whole = jnp.concatenate([a + b for a, b in sums], axis=1)
        return whole[:col_count]

    def put_vector(e, v, x):
        for s in range(capacity):
            asked = recv[0, pl.ds(per_vector + s, devices, stride=MSG), :]
            for h in range(halves):
                reply = jnp.zeros((devices, LANES), jnp.float32)
                for c in range(col_count):
                    reply = jnp.where(
                        asked == float(c), x[c : c + 1, h * LANES : (h + 1) * LANES], reply
                    )
                at = v * per_vector + h * capacity + s
                send[e, pl.ds(at, devices, stride=MSG), :] = reply

    def rounded(x):
        return x.astype(jnp.bfloat16).astype(jnp.float32)

    def lane_sum(x):
        x = jnp.sum(x * x, axis=0, keepdims=True)
        total = x[:, :LANES]
        for h in range(1, halves):
            total += x[:, h * LANES : (h + 1) * LANES]
        return total

    small_copies[0].wait()
    y = y_v[...]
    yb_v[...] = rounded(y)
    terms = adjoint(True)
    pl.semaphore_wait(barrier, devices - 1)
    send_terms(0, terms)
    for copy in small_copies[1:]:
        copy.wait()
    cost, upper, x = cost_v[...], upper_v[...], x_v[...]
    right = right_v[...]
    bounded = kind_v[...] == 1
    settle(recv, recv_sem, 0)
    put_vector(1, 1, rounded(x))
    col_image = column_image(0)
    last = 2 * ITERS + 1
    row_image = None
    for step in range(ITERS):
        out, back = 2 * step + 1, 2 * step + 2
        x_new = jnp.clip(x - PRIMAL_STEP * (cost - col_image), 0.0, upper)
        put_vector(out, 0, rounded(2.0 * x_new - x))
        exchange(out)
        settle(recv, recv_sem, out)
        images = forward(out)
        bar_image = images[:row_count]
        if step == 0:
            row_image = images[row_count : 2 * row_count]
        row_image = (bar_image + row_image) / 2.0
        y_new = y + DUAL_STEP * (right - bar_image)
        y_new = jnp.where(bounded, jnp.maximum(y_new, 0.0), y_new)
        yb_v[...] = rounded(y_new)
        send_terms(back, adjoint(False))
        violation = right - row_image
        violation = jnp.where(bounded, jnp.maximum(violation, 0.0), violation)
        send[last, 2 * step : 2 * step + 1, :] = lane_sum(violation)
        settle(recv, recv_sem, back)
        col_image = column_image(back)
        gap = x_new - jnp.clip(x_new - (cost - col_image), 0.0, upper)
        send[last, 2 * step + 1 : 2 * step + 2, :] = lane_sum(gap)
        x, y = x_new, y_new

    recv[last, 0:MSG, :] = send[last, 0:MSG, :]

    def tell(step):
        pltpu.make_async_remote_copy(
            src_ref=send.at[last, pl.ds(0, MSG)],
            dst_ref=recv.at[last, pl.ds(pl.multiple_of(MSG * (devices - step), MSG), MSG)],
            send_sem=send_sem.at[last],
            recv_sem=recv_sem.at[last],
            device_id={"rows": peer_of(step)},
            device_id_type=MESH,
        ).start()

    each_peer(tell)
    x_out[...] = x
    y_out[...] = y
    for e in range(last):
        settle(send, send_sem, e)
    settle(recv, recv_sem, last)
    sums = jnp.sum(recv[last].reshape(devices, MSG, LANES), axis=0)
    sums = jnp.sum(sums, axis=1, keepdims=True)
    kinds = lax.broadcasted_iota(jnp.int32, (MSG, 1), 0)
    row_scale = 1.0 / (row_count * devices * block)
    col_scale = 1.0 / (col_count * devices * block)
    scale = jnp.where(kinds % 2 == 0, row_scale, col_scale)
    roots = jnp.sqrt(sums * scale)
    side = lax.broadcasted_iota(jnp.int32, (1, 2), 1)
    for step in range(ITERS):
        norm_out[step : step + 1, :] = jnp.where(
            side == 0, roots[2 * step : 2 * step + 1], roots[2 * step + 1 : 2 * step + 2]
        )
    settle(send, send_sem, last)


def per_device(
    tiles,
    tile_rows,
    tile_cols,
    tile_count,
    right_side,
    row_kind,
    cost,
    upper,
    primal_init,
    dual_init,
):
    devices = lax.axis_size("rows")
    slots, block = tiles.shape[0], tiles.shape[1]
    span = MSG * devices
    exchanges = 2 * ITERS + 2
    f32, i32 = jnp.float32, jnp.int32
    smem = pl.BlockSpec(memory_space=pltpu.SMEM)
    anywhere = pl.BlockSpec(memory_space=pl.ANY)
    vmem = pl.BlockSpec(memory_space=pltpu.VMEM)
    places = devices * (-(-slots // devices))
    call = pl.pallas_call(
        functools.partial(kernel, devices),
        out_shape=(
            jax.ShapeDtypeStruct(primal_init.shape, f32),
            jax.ShapeDtypeStruct(dual_init.shape, f32),
            jax.ShapeDtypeStruct((ITERS, 2), f32),
        ),
        in_specs=[smem] * 3 + [anywhere] * 7,
        out_specs=(vmem, vmem, vmem),
        scratch_shapes=[
            pltpu.VMEM(tiles.shape, tiles.dtype),
            pltpu.VMEM(right_side.shape, f32),
            pltpu.VMEM(row_kind.shape, i32),
            pltpu.VMEM(cost.shape, f32),
            pltpu.VMEM(upper.shape, f32),
            pltpu.VMEM(primal_init.shape, f32),
            pltpu.VMEM(dual_init.shape, f32),
            pltpu.VMEM(dual_init.shape, f32),
            pltpu.VMEM((slots, LANES), i32),
            pltpu.VMEM((slots, LANES), i32),
            pltpu.VMEM((slots, LANES), i32),
            pltpu.VMEM((block // LANES, slots * 16, span), jnp.bfloat16),
            pltpu.VMEM((exchanges, span, LANES), f32),
            pltpu.VMEM((exchanges, span, LANES), f32),
            pltpu.SemaphoreType.DMA((6,)),
            pltpu.SemaphoreType.DMA((CHUNKS,)),
            pltpu.SemaphoreType.DMA((exchanges,)),
            pltpu.SemaphoreType.DMA((exchanges,)),
        ],
        compiler_params=pltpu.CompilerParams(
            collective_id=0, has_side_effects=True, vmem_limit_bytes=40 * 1024 * 1024
        ),
        name="pdhg",
    )
    return call(
        tile_rows,
        tile_cols,
        tile_count,
        tiles,
        right_side,
        row_kind,
        cost,
        upper,
        primal_init,
        dual_init,
    )


def solution(mesh):
    return jax.shard_map(
        per_device,
        mesh=mesh,
        in_specs=(
            P(("groups", "rows"), None, None),
            P(("groups", "rows")),
            P(("groups", "rows")),
            P(("groups", "rows")),
            P(("groups", "rows"), None),
            P(("groups", "rows"), None),
            P(("groups", "rows"), None),
            P(("groups", "rows"), None),
            P(("groups", "rows"), None),
            P(("groups", "rows"), None),
        ),
        out_specs=(P(("groups", "rows"), None), P(("groups", "rows"), None), P("groups", None)),
        check_vma=False,
    )
```

time: 126 us -> 50.2 us (0.40)
  blocking collectives: 39.7 us -> 0 us
  Pallas kernels: 0 us -> 39 us
  waiting for transfers between devices: 26.9 us -> 0 us
  starting transfers between devices: 26.2 us -> 0 us
  matrix products: 20.7 us -> 0 us
  local copies, waits for them, and re-layouts: 4.58 us -> 9.39 us
  between operations: 4.3 us -> 1.31 us
  other arithmetic: 2.33 us -> 0 us
    pallas_call x0 -> x1, Pallas kernels: none -> 39 us  [per_device(): call(tile_rows, tile_cols, tile_count, tiles, right_side, row_kind, cost,...]
    psum x1 -> x0, blocking collectives: 30.3 us -> none  [per_device(): dual_sum = lax.psum(dual_term, 'rows')]
    all_to_all x6 -> x0, waiting for transfers between devices: 26.9 us -> none  [the longest x3 15 us: spread_primal(): lax.all_to_all(reply, 'rows', split_axis=0, concat_axis=0, tiled=True)]
    all_to_all x6 -> x0, starting transfers between devices: 26.2 us -> none  [the longest x3 10.4 us: spread_primal(): lax.all_to_all(reply, 'rows', split_axis=0, concat_axis=0, tiled=True)]
    dot_general x24 -> x0, matrix products: 20.7 us -> none  [the longest x3 10.4 us: forward(): jnp.einsum('tij,tj->ti', tiles, picked, preferred_element_type=jnp.float32)]
    unnamed x22 -> x21, local copies, waits for them, and re-layouts: 0.05 us -> 9.39 us
    all_to_all x1 -> x0, blocking collectives: 9.33 us -> none  [column_image(): lax.all_to_all(outgoing, 'rows', split_axis=0, concat_axis=0, tiled=True)]
    all_to_all x13 -> x0, local copies, waits for them, and re-layouts: 3.75 us -> none  [the longest x6 1.89 us: spread_primal(): lax.all_to_all(reply, 'rows', split_axis=0, concat_axis=0, tiled=True)]
  transfers between devices with their start and end apart: 6 -> 0, of which waited for: 6 -> 0; matrix products, arithmetic and copies ran while one was open for 7% -> 0% of each run, Pallas kernels for 0% -> 0%
where the time goes in v1:
time: 50.2 us; the launch traced here: 49.7 us
  Pallas kernels  39 us (78%)
  local copies, waits for them, and re-layouts  9.39 us (19%)
  between operations  1.31 us (3%)
    pallas_call x1, Pallas kernels, per_device(): call(tile_rows, tile_cols, tile_count, tiles, right_side, row_kind, cost,...  39 us
    unnamed x21, local copies, waits for them, and re-layouts  9.39 us

profile of v1, /device:TPU:0, one launch (start us, length us, event | category | flops | bytes accessed | tf_op | source)
XLA Modules:
  0.0 49.7 jit_solution(3009717091263631983)
XLA Ops:
  1.3 0.0 copy-start
  1.3 2.2 %copy-done = bf16[32,256,256]{2,1,0:T(8,128)(2,1)S(1)} copy-done((bf16[32,256,256]{2,1,0:T(8,128)(2,1)S(1)}, bf16[32,256,256]{2,1,0:T(8,128)(2,1)}, u32[]{:S(2)}) %copy-start) | copy-done | bytes 4194328
  3.5 0.0 copy-start.1
  3.5 0.7 %copy-done.1 = f32[6,256]{1,0:T(8,128)S(1)} copy-done((f32[6,256]{1,0:T(8,128)S(1)}, f32[6,256]{1,0:T(8,128)}, u32[]{:S(2)}) %copy-start.1) | copy-done | bytes 6168
  4.2 0.0 copy-start.2
  4.2 0.7 %copy-done.2 = f32[6,256]{1,0:T(8,128)S(1)} copy-done((f32[6,256]{1,0:T(8,128)S(1)}, f32[6,256]{1,0:T(8,128)}, u32[]{:S(2)}) %copy-start.2) | copy-done | bytes 6168
  4.9 0.0 copy-start.3
  4.9 0.7 %copy-done.3 = f32[6,256]{1,0:T(8,128)S(1)} copy-done((f32[6,256]{1,0:T(8,128)S(1)}, f32[6,256]{1,0:T(8,128)}, u32[]{:S(2)}) %copy-start.3) | copy-done | bytes 6168
  5.6 0.0 copy-start.4
  5.6 0.7 %copy-done.4 = f32[4,256]{1,0:T(4,128)S(1)} copy-done((f32[4,256]{1,0:T(4,128)S(1)}, f32[4,256]{1,0:T(4,128)}, u32[]{:S(2)}) %copy-start.4) | copy-done | bytes 4120
  6.2 0.0 copy-start.5
  6.2 0.7 %copy-done.5 = s32[4,256]{1,0:T(4,128)S(1)} copy-done((s32[4,256]{1,0:T(4,128)S(1)}, s32[4,256]{1,0:T(4,128)}, u32[]{:S(2)}) %copy-start.5) | copy-done | bytes 4120
  6.9 0.0 copy-start.6
  6.9 0.7 %copy-done.6 = f32[4,256]{1,0:T(4,128)S(1)} copy-done((f32[4,256]{1,0:T(4,128)S(1)}, f32[4,256]{1,0:T(4,128)}, u32[]{:S(2)}) %copy-start.6) | copy-done | bytes 4120
  7.6 0.0 copy-start.7
  7.6 0.7 %copy-done.7 = s32[32]{0:T(128)S(1)} copy-done((s32[32]{0:T(128)S(1)}, s32[32]{0:T(128)}, u32[]{:S(2)}) %copy-start.7) | copy-done | bytes 152
  8.3 0.0 copy-start.8
  8.3 0.7 %copy-done.8 = s32[32]{0:T(128)S(1)} copy-done((s32[32]{0:T(128)S(1)}, s32[32]{0:T(128)}, u32[]{:S(2)}) %copy-start.8) | copy-done | bytes 152
  8.9 39.0 %pdhg.1 = (f32[6,256]{1,0:T(8,128)S(1)}, f32[4,256]{1,0:T(4,128)S(1)}, f32[2,2]{1,0:T(2,128)S(1)}) custom-call(s32[32]{0:T(128)S(1)} %copy-done.7, s32[32]{0:T(128)S(1)} %copy-done.8, s32[1]{0:T(128)S(6)} %copy.16.count_s, bf16[32,256,256]{2,1,0:T(8,128)(2,1)S(1)} %copy-done, f32[4,256]{1,0:T(4,128)S(1)} %copy-done.4, s32[4,256]{1,0:T(4,128)S(1)} %copy-done.5, ...), custom_call_target="tpu_custom_call" | custom-call | tf_op jit(solution)/shard_map/pdhg/pallas_call | solution.py:391
  48.0 0.6 %copy.17 = f32[6,256]{1,0:T(8,128)} copy(f32[6,256]{1,0:T(8,128)S(1)} %get-tuple-element.6) | data formatting | bytes 12288
  48.6 0.6 %copy.18 = f32[4,256]{1,0:T(4,128)} copy(f32[4,256]{1,0:T(4,128)S(1)} %get-tuple-element.7) | data formatting | bytes 8192
  49.2 0.6 %copy.19 = f32[2,2]{1,0:T(2,128)} copy(f32[2,2]{1,0:T(2,128)S(1)} %get-tuple-element.8) | data formatting | bytes 32
Async XLA Ops:
  1.3 2.2 %copy-start = (bf16[32,256,256]{2,1,0:T(8,128)(2,1)S(1)}, bf16[32,256,256]{2,1,0:T(8,128)(2,1)}, u32[]{:S(2)}) copy-start(bf16[32,256,256]{2,1,0:T(8,128)(2,1)} %tiles_h.1) | copy-start | bytes 12582916
  3.5 0.7 %copy-start.1 = (f32[6,256]{1,0:T(8,128)S(1)}, f32[6,256]{1,0:T(8,128)}, u32[]{:S(2)}) copy-start(f32[6,256]{1,0:T(8,128)} %cost_h.1) | copy-start | bytes 18436
  4.2 0.7 %copy-start.2 = (f32[6,256]{1,0:T(8,128)S(1)}, f32[6,256]{1,0:T(8,128)}, u32[]{:S(2)}) copy-start(f32[6,256]{1,0:T(8,128)} %upper_h.1) | copy-start | bytes 18436
  4.9 0.7 %copy-start.3 = (f32[6,256]{1,0:T(8,128)S(1)}, f32[6,256]{1,0:T(8,128)}, u32[]{:S(2)}) copy-start(f32[6,256]{1,0:T(8,128)} %x_h.1) | copy-start | bytes 18436
  5.6 0.7 %copy-start.4 = (f32[4,256]{1,0:T(4,128)S(1)}, f32[4,256]{1,0:T(4,128)}, u32[]{:S(2)}) copy-start(f32[4,256]{1,0:T(4,128)} %right_h.1) | copy-start | bytes 12292
  6.2 0.7 %copy-start.5 = (s32[4,256]{1,0:T(4,128)S(1)}, s32[4,256]{1,0:T(4,128)}, u32[]{:S(2)}) copy-start(s32[4,256]{1,0:T(4,128)} %kind_h.1) | copy-start | bytes 12292
  6.9 0.7 %copy-start.6 = (f32[4,256]{1,0:T(4,128)S(1)}, f32[4,256]{1,0:T(4,128)}, u32[]{:S(2)}) copy-start(f32[4,256]{1,0:T(4,128)} %y_h.1) | copy-start | bytes 12292
  7.6 0.7 %copy-start.7 = (s32[32]{0:T(128)S(1)}, s32[32]{0:T(128)}, u32[]{:S(2)}) copy-start(s32[32]{0:T(128)} %rows_s.1) | copy-start | bytes 388
  8.3 0.7 %copy-start.8 = (s32[32]{0:T(128)S(1)}, s32[32]{0:T(128)}, u32[]{:S(2)}) copy-start(s32[32]{0:T(128)} %cols_s.1) | copy-start | bytes 388

commit v2 on v1

--- a/solution.py
+++ b/solution.py
@@ -18,9 +18,9 @@
 
 def kernel(
     devices,
-    rows_s,
-    cols_s,
-    count_s,
+    rows_h,
+    cols_h,
+    count_h,
     tiles_h,
     right_h,
     kind_h,
@@ -31,7 +31,11 @@
     x_out,
     y_out,
     norm_out,
+    rows_s,
+    cols_s,
+    count_s,
     tiles_v,
+    flipped_v,
     right_v,
     kind_v,
     cost_v,
@@ -60,15 +64,32 @@
     per_chunk = slots // CHUNKS
     me = lax.axis_index("rows")
 
+    bits = devices.bit_length() - 1
+    if devices != 1 << bits or per_vector * 2 > MSG or col_count > MSG:
+        raise ValueError("unsupported sizes")
+
     def peer_of(step):
-        return lax.rem(me + step, devices)
+        peer = me
+        for b in range(bits):
+            one = 1 << b
+            peer += ((step // one) % 2) * one * (1 - 2 * ((me // one) % 2))
+        return peer
 
     def each_peer(do):
         if devices <= 16:
-            for step in range(1, devices):
+            for step in reversed(range(1, devices)):
                 do(step)
         else:
-            pl.loop(1, devices)(do)
+            pl.loop(0, devices - 1)(lambda i: do(devices - 1 - i))
+
+    barrier = pltpu.get_barrier_semaphore()
+
+    def greet(step):
+        pl.semaphore_signal(
+            barrier, inc=1, device_id={"rows": peer_of(step)}, device_id_type=MESH
+        )
+
+    each_peer(greet)
 
     chunk_copies = []
     for c in range(CHUNKS):
@@ -78,6 +99,9 @@
         )
     small_copies = []
     pairs = (
+        (cols_h, cols_s),
+        (count_h, count_s),
+        (rows_h, rows_s),
         (y_h, y_v),
         (cost_h, cost_v),
         (upper_h, upper_v),
@@ -87,20 +111,15 @@
     )
     for n, (src, dst) in enumerate(pairs):
         small_copies.append(pltpu.make_async_copy(src, dst, small_sem.at[n]))
-    small_copies[0].start()
+    for copy in small_copies[:4]:
+        copy.start()
     for copy in chunk_copies:
         copy.start()
-    for copy in small_copies[1:]:
+    for copy in small_copies[4:]:
         copy.start()
 
-    barrier = pltpu.get_barrier_semaphore()
-
-    def greet(step):
-        pl.semaphore_signal(
-            barrier, inc=1, device_id={"rows": peer_of(step)}, device_id_type=MESH
-        )
-
-    each_peer(greet)
+    for copy in small_copies[:3]:
+        copy.wait()
 
     lane = lax.broadcasted_iota(jnp.int32, (slots, LANES), 1)
     sub = lax.broadcasted_iota(jnp.int32, (slots, LANES), 0)
@@ -111,8 +130,10 @@
         col = cols_s[t]
         owner = col // col_count
         local = col - owner * col_count
-        step = owner - me
-        step = jnp.where(step < 0, step + devices, step)
+        step = 0
+        for b in range(bits):
+            one = 1 << b
+            step += ((owner // one + me // one) % 2) * one
         step = jnp.where(t < count_s[0], step, 16 * devices + t)
         peer_v[t : t + 1, :] = jnp.full((1, LANES), step, jnp.int32)
         peer_l = jnp.where(lane1 == t, step, peer_l)
@@ -134,7 +155,6 @@
         jnp.where(found, (local_l + 1).astype(jnp.float32), 0.0), axis=1, keepdims=True
     )
     col_of = jnp.broadcast_to(col_of - 1.0, (places, LANES))
-    send[...] = jnp.zeros_like(send)
     for s in range(capacity):
         send[0, pl.ds(per_vector + s, devices, stride=MSG), :] = col_of[
             s * devices : (s + 1) * devices
@@ -178,8 +198,10 @@
             total += jnp.dot(left, right, preferred_element_type=jnp.float32)
         return total
 
+    message_row = lax.broadcasted_iota(jnp.int32, (span, LANES), 0) % MSG
+
     def forward(e):
-        arrived = recv[e].astype(jnp.bfloat16)
+        arrived = jnp.where(message_row < used[e], recv[e], 0.0).astype(jnp.bfloat16)
         picked = [
             jnp.dot(pick_v[h], arrived, preferred_element_type=jnp.float32).astype(
                 jnp.bfloat16
@@ -187,20 +209,27 @@
             for h in range(halves)
         ]
         total = jnp.zeros((16, block), jnp.float32)
-        for t in range(slots):
-            left = jnp.concatenate([p[t * 16 : (t + 1) * 16] for p in picked], axis=1)
-            total += lax.dot_general(
-                left, tiles_v[t], (((1,), (1,)), ((), ())), preferred_element_type=jnp.float32
+        for c in range(CHUNKS):
+            parts = []
+            for t in range(c * per_chunk, (c + 1) * per_chunk):
+                parts += [p[t * 16 : (t + 1) * 16] for p in picked]
+            left = jnp.concatenate(parts, axis=1)
+            right = flipped_v[c * per_chunk : (c + 1) * per_chunk].reshape(
+                per_chunk * block, block
             )
+            total += jnp.dot(left, right, preferred_element_type=jnp.float32)
         return total
 
+    used = [per_vector] * (2 * ITERS + 2)
+    used[0], used[1], used[-1] = per_vector + capacity, 2 * per_vector, 2 * ITERS
+
     def exchange(e):
-        recv[e, 0:MSG, :] = send[e, 0:MSG, :]
+        recv[e, 0 : used[e], :] = send[e, 0 : used[e], :]
 
         def go(step):
             pltpu.make_async_remote_copy(
-                src_ref=send.at[e, pl.ds(pl.multiple_of(MSG * step, MSG), MSG)],
-                dst_ref=recv.at[e, pl.ds(pl.multiple_of(MSG * (devices - step), MSG), MSG)],
+                src_ref=send.at[e, pl.ds(pl.multiple_of(MSG * step, MSG), used[e])],
+                dst_ref=recv.at[e, pl.ds(pl.multiple_of(MSG * step, MSG), used[e])],
                 send_sem=send_sem.at[e],
                 recv_sem=recv_sem.at[e],
                 device_id={"rows": peer_of(step)},
@@ -210,7 +239,7 @@
         each_peer(go)
 
     def settle(buffer, sems, e):
-        rest = buffer.at[e, pl.ds(MSG, span - MSG)]
+        rest = buffer.at[e, pl.ds(MSG, (devices - 1) * used[e])]
         pltpu.make_async_copy(rest, rest, sems.at[e]).wait()
 
     def send_terms(e, terms):
@@ -260,13 +289,15 @@
             total += x[:, h * LANES : (h + 1) * LANES]
         return total
 
-    small_copies[0].wait()
+    small_copies[3].wait()
     y = y_v[...]
     yb_v[...] = rounded(y)
     terms = adjoint(True)
     pl.semaphore_wait(barrier, devices - 1)
     send_terms(0, terms)
-    for copy in small_copies[1:]:
+    for t in range(slots):
+        flipped_v[t] = tiles_v[t].T
+    for copy in small_copies[4:]:
         copy.wait()
     cost, upper, x = cost_v[...], upper_v[...], x_v[...]
     right = right_v[...]
@@ -300,12 +331,12 @@
         send[last, 2 * step + 1 : 2 * step + 2, :] = lane_sum(gap)
         x, y = x_new, y_new
 
-    recv[last, 0:MSG, :] = send[last, 0:MSG, :]
+    recv[last, 0 : used[last], :] = send[last, 0 : used[last], :]
 
     def tell(step):
         pltpu.make_async_remote_copy(
-            src_ref=send.at[last, pl.ds(0, MSG)],
-            dst_ref=recv.at[last, pl.ds(pl.multiple_of(MSG * (devices - step), MSG), MSG)],
+            src_ref=send.at[last, pl.ds(0, used[last])],
+            dst_ref=recv.at[last, pl.ds(pl.multiple_of(MSG * step, MSG), used[last])],
             send_sem=send_sem.at[last],
             recv_sem=recv_sem.at[last],
             device_id={"rows": peer_of(step)},
@@ -350,7 +381,6 @@
     span = MSG * devices
     exchanges = 2 * ITERS + 2
     f32, i32 = jnp.float32, jnp.int32
-    smem = pl.BlockSpec(memory_space=pltpu.SMEM)
     anywhere = pl.BlockSpec(memory_space=pl.ANY)
     vmem = pl.BlockSpec(memory_space=pltpu.VMEM)
     places = devices * (-(-slots // devices))
@@ -361,9 +391,13 @@
             jax.ShapeDtypeStruct(dual_init.shape, f32),
             jax.ShapeDtypeStruct((ITERS, 2), f32),
         ),
-        in_specs=[smem] * 3 + [anywhere] * 7,
+        in_specs=[anywhere] * 10,
         out_specs=(vmem, vmem, vmem),
         scratch_shapes=[
+            pltpu.SMEM(tile_rows.shape, i32),
+            pltpu.SMEM(tile_cols.shape, i32),
+            pltpu.SMEM(tile_count.shape, i32),
+            pltpu.VMEM(tiles.shape, tiles.dtype),
             pltpu.VMEM(tiles.shape, tiles.dtype),
             pltpu.VMEM(right_side.shape, f32),
             pltpu.VMEM(row_kind.shape, i32),
@@ -378,13 +412,13 @@
             pltpu.VMEM((block // LANES, slots * 16, span), jnp.bfloat16),
             pltpu.VMEM((exchanges, span, LANES), f32),
             pltpu.VMEM((exchanges, span, LANES), f32),
-            pltpu.SemaphoreType.DMA((6,)),
+            pltpu.SemaphoreType.DMA((9,)),
             pltpu.SemaphoreType.DMA((CHUNKS,)),
             pltpu.SemaphoreType.DMA((exchanges,)),
             pltpu.SemaphoreType.DMA((exchanges,)),
         ],
         compiler_params=pltpu.CompilerParams(
-            collective_id=0, has_side_effects=True, vmem_limit_bytes=40 * 1024 * 1024
+            collective_id=0, has_side_effects=True, vmem_limit_bytes=64 * 1024 * 1024
         ),
         name="pdhg",
     )

time: 50.2 us -> 41.3 us (0.82)
  local copies, waits for them, and re-layouts: 9.39 us -> 3.79 us
  Pallas kernels: 39 us -> 36 us
    unnamed x21 -> x3, local copies, waits for them, and re-layouts: 9.39 us -> 3.79 us
    pallas_call x1, Pallas kernels: 39 us -> 36 us  [per_device(): call(tile_rows, tile_cols, tile_count, tiles, right_side, row_kind, cost,...]
where the time goes in v2:
time: 41.3 us; the launch traced here: 41.1 us
  Pallas kernels  36 us (87%)
  local copies, waits for them, and re-layouts  3.79 us (9%)
  between operations  1.29 us (3%)
    pallas_call x1, Pallas kernels, per_device(): call(tile_rows, tile_cols, tile_count, tiles, right_side, row_kind, cost,...  36 us
    unnamed x3, local copies, waits for them, and re-layouts  3.79 us

profile of v2, /device:TPU:0, one launch (start us, length us, event | category | flops | bytes accessed | tf_op | source)
XLA Modules:
  0.0 41.1 jit_solution(5213775609114422644)
XLA Ops:
  1.3 36.0 %pdhg.1 = (f32[6,256]{1,0:T(8,128)}, f32[4,256]{1,0:T(4,128)}, f32[2,2]{1,0:T(2,128)}) custom-call(s32[32]{0:T(128)} %rows_h.1, s32[32]{0:T(128)} %cols_h.1, s32[1]{0:T(128)S(6)} %copy.16.count_h, bf16[32,256,256]{2,1,0:T(8,128)(2,1)} %tiles_h.1, f32[4,256]{1,0:T(4,128)} %right_h.1, s32[4,256]{1,0:T(4,128)} %kind_h.1, f32[6,256]{1,0:T(8,128)} %cost_h.1, ...), custom_call_target="tpu_custom_call" | custom-call | tf_op jit(solution)/shard_map/pdhg/pallas_call | solution.py:425
  37.3 1.3 %copy.17 = f32[6,256]{1,0:T(8,128)} copy(f32[6,256]{1,0:T(8,128)} %get-tuple-element.6) | data formatting | bytes 12288
  38.6 1.3 %copy.18 = f32[4,256]{1,0:T(4,128)} copy(f32[4,256]{1,0:T(4,128)} %get-tuple-element.7) | data formatting | bytes 8192
  39.9 1.2 %copy.19 = f32[2,2]{1,0:T(2,128)} copy(f32[2,2]{1,0:T(2,128)} %get-tuple-element.8) | data formatting | bytes 32

commit v3 on v2

--- a/solution.py
+++ b/solution.py
@@ -28,9 +28,7 @@
     upper_h,
     x_h,
     y_h,
-    x_out,
-    y_out,
-    norm_out,
+    packed_out,
     rows_s,
     cols_s,
     count_s,
@@ -344,8 +342,8 @@
         ).start()
 
     each_peer(tell)
-    x_out[...] = x
-    y_out[...] = y
+    packed_out[0:col_count, :] = x
+    packed_out[MSG : MSG + row_count, :] = y
     for e in range(last):
         settle(send, send_sem, e)
     settle(recv, recv_sem, last)
@@ -356,12 +354,18 @@
     col_scale = 1.0 / (col_count * devices * block)
     scale = jnp.where(kinds % 2 == 0, row_scale, col_scale)
     roots = jnp.sqrt(sums * scale)
-    side = lax.broadcasted_iota(jnp.int32, (1, 2), 1)
+    side = lax.broadcasted_iota(jnp.int32, (1, LANES), 1)
     for step in range(ITERS):
-        norm_out[step : step + 1, :] = jnp.where(
+        packed_out[2 * MSG + step : 2 * MSG + step + 1, :LANES] = jnp.where(
             side == 0, roots[2 * step : 2 * step + 1], roots[2 * step + 1 : 2 * step + 2]
         )
     settle(send, send_sem, last)
+
+
+def unpack(packed, x_out, y_out, norm_out):
+    x_out[...] = packed[: x_out.shape[0]]
+    y_out[...] = packed[MSG : MSG + y_out.shape[0]]
+    norm_out[...] = packed[2 * MSG : 2 * MSG + ITERS, :2]
 
 
 def per_device(
@@ -386,13 +390,9 @@
     places = devices * (-(-slots // devices))
     call = pl.pallas_call(
         functools.partial(kernel, devices),
-        out_shape=(
-            jax.ShapeDtypeStruct(primal_init.shape, f32),
-            jax.ShapeDtypeStruct(dual_init.shape, f32),
-            jax.ShapeDtypeStruct((ITERS, 2), f32),
-        ),
+        out_shape=jax.ShapeDtypeStruct((3 * MSG, block), f32),
         in_specs=[anywhere] * 10,
-        out_specs=(vmem, vmem, vmem),
+        out_specs=vmem,
         scratch_shapes=[
             pltpu.SMEM(tile_rows.shape, i32),
             pltpu.SMEM(tile_cols.shape, i32),
@@ -422,7 +422,7 @@
         ),
         name="pdhg",
     )
-    return call(
+    packed = call(
         tile_rows,
         tile_cols,
         tile_count,
@@ -434,6 +434,17 @@
         primal_init,
         dual_init,
     )
+    return pl.pallas_call(
+        unpack,
+        out_shape=(
+            jax.ShapeDtypeStruct(primal_init.shape, f32),
+            jax.ShapeDtypeStruct(dual_init.shape, f32),
+            jax.ShapeDtypeStruct((ITERS, 2), f32),
+        ),
+        in_specs=[vmem],
+        out_specs=(vmem, vmem, vmem),
+        name="unpack",
+    )(packed)
 
 
 def solution(mesh):

time: 41.3 us -> 38.8 us (0.939)
  local copies, waits for them, and re-layouts: 3.79 us -> 0 us
  Pallas kernels: 36 us -> 37.3 us
    unnamed x3 -> x0, local copies, waits for them, and re-layouts: 3.79 us -> none
    pallas_call x0 -> x1, Pallas kernels: none -> 1.34 us  [per_device(): pl.pallas_call(unpack, out_shape=(jax.ShapeDtypeStruct(primal_init.shape,...]
where the time goes in v3:
time: 38.8 us; the launch traced here: 38.6 us
  Pallas kernels  37.3 us (96%)
  between operations  1.29 us (3%)
    pallas_call x1, Pallas kernels, per_device(): call(tile_rows, tile_cols, tile_count, tiles, right_side, row_kind, cost,...  36 us
    pallas_call x1, Pallas kernels, per_device(): pl.pallas_call(unpack, out_shape=(jax.ShapeDtypeStruct(primal_init.shape,...  1.34 us

profile of v3, /device:TPU:0, one launch (start us, length us, event | category | flops | bytes accessed | tf_op | source)
XLA Modules:
  0.0 38.6 jit_solution(17442645094389315016)
XLA Ops:
  1.3 36.0 %pdhg.1.packed = f32[24,256]{1,0:T(8,128)} custom-call(s32[32]{0:T(128)} %rows_h.1, s32[32]{0:T(128)} %cols_h.1, s32[1]{0:T(128)S(6)} %copy.13.count_h, bf16[32,256,256]{2,1,0:T(8,128)(2,1)} %tiles_h.1, f32[4,256]{1,0:T(4,128)} %right_h.1, s32[4,256]{1,0:T(4,128)} %kind_h.1, f32[6,256]{1,0:T(8,128)} %cost_h.1, f32[6,256]{1,0:T(8,128)} %upper_h.1, ...), custom_call_target="tpu_custom_call" | custom-call | tf_op jit(solution)/shard_map/pdhg/pallas_call | solution.py:425
  37.3 1.3 %unpack.1 = (f32[6,256]{1,0:T(8,128)}, f32[4,256]{1,0:T(4,128)}, f32[2,2]{1,0:T(2,128)}) custom-call(f32[24,256]{1,0:T(8,128)} %pdhg.1.packed), custom_call_target="tpu_custom_call" | custom-call | tf_op jit(solution)/shard_map/unpack/pallas_call | solution.py:437

commit v4 on v3

--- a/solution.py
+++ b/solution.py
@@ -158,22 +158,6 @@
             s * devices : (s + 1) * devices
         ]
 
-    wide_lane = lax.broadcasted_iota(jnp.int32, (16, span), 1)
-    wide_sub = lax.broadcasted_iota(jnp.int32, (16, span), 0)
-    vector_of = wide_sub // row_count
-    row_of = jnp.where(vector_of < 2, wide_sub - vector_of * row_count, -1)
-    wanted = wide_lane - vector_of * per_vector
-    for t in range(slots):
-        base = base_v[t : t + 1, :]
-        if span > LANES:
-            base = jnp.concatenate([base] * (span // LANES), axis=1)
-        hit_row = row_of == rows_s[t]
-        for h in range(halves):
-            hit = hit_row & (wanted == base + h * capacity)
-            pick_v[h, t * 16 : (t + 1) * 16, :] = jnp.where(hit, 1.0, 0.0).astype(
-                jnp.bfloat16
-            )
-
     place_wide = lax.broadcasted_iota(jnp.int32, (places, block), 0)
 
     def adjoint(first):
@@ -293,6 +277,23 @@
     terms = adjoint(True)
     pl.semaphore_wait(barrier, devices - 1)
     send_terms(0, terms)
+
+    wide_lane = lax.broadcasted_iota(jnp.int32, (16, span), 1)
+    wide_sub = lax.broadcasted_iota(jnp.int32, (16, span), 0)
+    vector_of = wide_sub // row_count
+    row_of = jnp.where(vector_of < 2, wide_sub - vector_of * row_count, -1)
+    wanted = wide_lane - vector_of * per_vector
+    for t in range(slots):
+        base = base_v[t : t + 1, :]
+        if span > LANES:
+            base = jnp.concatenate([base] * (span // LANES), axis=1)
+        hit_row = row_of == rows_s[t]
+        for h in range(halves):
+            hit = hit_row & (wanted == base + h * capacity)
+            pick_v[h, t * 16 : (t + 1) * 16, :] = jnp.where(hit, 1.0, 0.0).astype(
+                jnp.bfloat16
+            )
+
     for t in range(slots):
         flipped_v[t] = tiles_v[t].T
     for copy in small_copies[4:]:

time: 38.8 us -> 38.8 us (level)
  no operation moved by 1% of the time
where the time goes in v4:
time: 38.8 us; the launch traced here: 38.6 us
  Pallas kernels  37.3 us (96%)
  between operations  1.29 us (3%)
    pallas_call x1, Pallas kernels, per_device(): call(tile_rows, tile_cols, tile_count, tiles, right_side, row_kind, cost,...  36 us
    pallas_call x1, Pallas kernels, per_device(): pl.pallas_call(unpack, out_shape=(jax.ShapeDtypeStruct(primal_init.shape,...  1.34 us

profile of v4, /device:TPU:0, one launch (start us, length us, event | category | flops | bytes accessed | tf_op | source)
XLA Modules:
  0.0 38.6 jit_solution(2729161761438881702)
XLA Ops:
  1.3 36.0 %pdhg.1.packed = f32[24,256]{1,0:T(8,128)} custom-call(s32[32]{0:T(128)} %rows_h.1, s32[32]{0:T(128)} %cols_h.1, s32[1]{0:T(128)S(6)} %copy.13.count_h, bf16[32,256,256]{2,1,0:T(8,128)(2,1)} %tiles_h.1, f32[4,256]{1,0:T(4,128)} %right_h.1, s32[4,256]{1,0:T(4,128)} %kind_h.1, f32[6,256]{1,0:T(8,128)} %cost_h.1, f32[6,256]{1,0:T(8,128)} %upper_h.1, ...), custom_call_target="tpu_custom_call" | custom-call | tf_op jit(solution)/shard_map/pdhg/pallas_call | solution.py:426
  37.3 1.3 %unpack.1 = (f32[6,256]{1,0:T(8,128)}, f32[4,256]{1,0:T(4,128)}, f32[2,2]{1,0:T(2,128)}) custom-call(f32[24,256]{1,0:T(8,128)} %pdhg.1.packed), custom_call_target="tpu_custom_call" | custom-call | tf_op jit(solution)/shard_map/unpack/pallas_call | solution.py:438
